TPU v7x, 512 devices: a whole 4x4x16 slice. The times are simulated.
512 devices in a mesh: dp: 16 (over y, x), expert: 32 (over z, core).
Axes of the slice: x: 4, y: 4, z: 16, core: 2. Of those that a mesh axis runs over, the one named last changes fastest.
Arguments:
- tokens: bfloat16 [65536, 512], P(('dp', 'expert')), may hold values from -6 to 6
- cotangent: bfloat16 [65536, 512], P(('dp', 'expert')), may hold values from -0.29882812 to 0.29882812
- labels: int32 [65536, 1], P(('dp', 'expert')), may hold values from 0 to 63; in each aligned block of 128 rows (0 to 127, 128 to 255, ...) at most 4 rows name the same one
- placement: int32 [64], replicated, may hold values from 0 to 63, each once
- mass: float32 [65536], P(('dp', 'expert')), may hold values from 0.1 to 10
- w_head: float32 [512, 16], replicated, may hold values from -0.25 to 0.25
- w_up: bfloat16 [64, 512, 2048], P('expert', None, 'dp'), may hold values from -0.25 to 0.25
- w_down: bfloat16 [64, 2048, 512], P('expert', 'dp'), may hold values from -0.125 to 0.125
- up_moment: bfloat16 [64, 512, 2048], P('expert', None, 'dp'), may hold values from -2 to 2
- up_square: bfloat16 [64, 512, 2048], P('expert', None, 'dp'), may hold values from 0.0099487305 to 1
- down_moment: bfloat16 [64, 2048, 512], P('expert', 'dp'), may hold values from -2 to 2
- down_square: bfloat16 [64, 2048, 512], P('expert', 'dp'), may hold values from 0.0099487305 to 1
Outputs:
- fine_precip: float32 [65536, 16], P(('dp', 'expert'))
- up_next: bfloat16 [64, 512, 2048], P('expert', None, 'dp')
- down_next: bfloat16 [64, 2048, 512], P('expert', 'dp')
- up_moment_next: bfloat16 [64, 512, 2048], P('expert', None, 'dp')
- up_square_next: bfloat16 [64, 512, 2048], P('expert', None, 'dp')
- down_moment_next: bfloat16 [64, 2048, 512], P('expert', 'dp')
- down_square_next: bfloat16 [64, 2048, 512], P('expert', 'dp')
Inputs may be any that keep to these rules, and one draw needn't show every extreme that they name: `labels`: within each device's block of 128 rows no regime is named more than 4 times, and in every draw some regime is named exactly 4 times in some block; every regime is named somewhere. `placement`: each regime stands in exactly one expert slot.
All inputs are finite; a program needn't handle non-finite values.
Results may differ from a plain program's by a relative error of at most 0.0045.
Values may be sent and summed in bfloat16 or wider, within the bound.
A program may use at most 64 MiB of HBM per device.

v0:
```python
import jax
import jax.numpy as jnp
from jax import lax
from jax.sharding import PartitionSpec as P

CAP = 4
beta_first = 0.9
beta_second = 0.95
correct_first = 1.0 - 0.9**20
correct_second = 1.0 - 0.95**20
learn_rate = 0.002
adam_epsilon = 1e-08


def gelu_parts(pre):
    normal_cdf = 0.5 * (1.0 + lax.erf(pre * 0.7071067811865476))
    density = jnp.exp(-0.5 * pre * pre) * 0.3989422804014327
    return (pre * normal_cdf, normal_cdf + pre * density)


def adam_step(weight, first, second, grad):
    new_first = beta_first * first.astype(jnp.float32) + (1.0 - beta_first) * grad
    new_second = beta_second * second.astype(jnp.float32) + (1.0 - beta_second) * grad * grad
    update = new_first / correct_first / (jnp.sqrt(new_second / correct_second) + adam_epsilon)
    moved = weight.astype(jnp.float32) - learn_rate * update
    return (
        moved.astype(jnp.bfloat16),
        new_first.astype(jnp.bfloat16),
        new_second.astype(jnp.bfloat16),
    )


def route_slots(labels, placement, capacity, holders, local_count):
    experts = placement.shape[0]
    regimes = jnp.arange(experts, dtype=jnp.int32)
    owner = jnp.sum(jnp.where(placement[None, :] == regimes[:, None], regimes[None, :], 0), axis=1)
    chosen = labels[:, 0][:, None] == regimes[None, :]
    target = jnp.sum(jnp.where(chosen, owner[None, :], 0), axis=1)
    onehot = (target[:, None] == regimes[None, :]).astype(jnp.int32)
    earlier = jnp.cumsum(onehot, axis=0) - onehot
    position = jnp.sum(earlier * onehot, axis=1)
    lane_index = target % local_count * holders + target // local_count
    return lane_index * capacity + position


def fill_slots(values, slots, count):
    row_count = values.shape[0]
    source = (
        jnp.full((count,), row_count, jnp.int32)
        .at[slots]
        .set(jnp.arange(row_count, dtype=jnp.int32))
    )
    padded = jnp.concatenate([values, jnp.zeros((1, values.shape[1]), values.dtype)], axis=0)
    return jnp.take(padded, source, axis=0)


def expert_rows(rows_x, rows_grad, w_in, w_out):
    pre = jnp.einsum("krd,kdf->krf", rows_x, w_in, preferred_element_type=jnp.float32)
    value, slope = gelu_parts(pre)
    hidden = value.astype(jnp.bfloat16)
    back = jnp.einsum("krd,kfd->krf", rows_grad, w_out, preferred_element_type=jnp.float32)
    hidden_grad = (back * slope).astype(jnp.bfloat16)
    return (hidden, hidden_grad)


def outer_in(rows_x, hidden_grad):
    return jnp.einsum("krd,krf->kdf", rows_x, hidden_grad, preferred_element_type=jnp.float32)


def outer_out(hidden, rows_grad):
    return jnp.einsum("krf,krd->kfd", hidden, rows_grad, preferred_element_type=jnp.float32)


def local(
    tokens,
    cotangent,
    labels,
    placement,
    mass,
    w_head,
    w_up,
    w_down,
    up_moment,
    up_square,
    down_moment,
    down_square,
):
    capacity = CAP
    experts = placement.shape[0]
    width = tokens.shape[1]
    local_count = w_up.shape[0]
    holders = lax.axis_size("expert")
    slots = route_slots(labels, placement, capacity, holders, local_count)
    slot_count = experts * capacity
    recv_rows = holders * capacity
    send_x = fill_slots(tokens, slots, slot_count).reshape(local_count, holders, capacity, width)
    send_grad = fill_slots(cotangent, slots, slot_count).reshape(
        local_count, holders, capacity, width
    )
    recv_x, recv_grad = (
        lax.all_to_all(send_x, "expert", split_axis=1, concat_axis=1, tiled=True),
        lax.all_to_all(send_grad, "expert", split_axis=1, concat_axis=1, tiled=True),
    )
    recv_x = recv_x.reshape(local_count, recv_rows, width)
    recv_grad = recv_grad.reshape(local_count, recv_rows, width)
    piece_x = lax.all_gather(recv_x, "dp", axis=1, tiled=True)
    piece_grad = lax.all_gather(recv_grad, "dp", axis=1, tiled=True)
    hidden, hidden_grad = expert_rows(piece_x, piece_grad, w_up, w_down)
    grad_in = outer_in(piece_x, hidden_grad)
    grad_out = outer_out(hidden, piece_grad)
    absorb_hidden_all = jnp.swapaxes(hidden, 0, 1)
    hidden_all, grad_in, grad_out = (absorb_hidden_all, grad_in, grad_out)
    summed = lax.psum_scatter(
        jnp.einsum("rkf,kfd->rkd", hidden_all, w_down, preferred_element_type=jnp.float32).astype(
            jnp.bfloat16
        ),
        "dp",
        scatter_dimension=0,
        tiled=True,
    )
    outgoing = jnp.swapaxes(summed, 0, 1).reshape(local_count, holders, capacity, width)
    returned = lax.all_to_all(outgoing, "expert", split_axis=1, concat_axis=1, tiled=True)
    expert_out = jnp.take(returned.reshape(slot_count, width), slots, axis=0)
    field = tokens.astype(jnp.float32) + expert_out.astype(jnp.float32)
    logits = jnp.dot(
        field, w_head, precision=lax.Precision.HIGHEST, preferred_element_type=jnp.float32
    )
    positive = jax.nn.softplus(logits) + 0.1
    fine_precip = mass[:, None] * positive / jnp.sum(positive, axis=1, keepdims=True)
    up_next, up_moment_next, up_square_next = adam_step(w_up, up_moment, up_square, grad_in)
    down_next, down_moment_next, down_square_next = adam_step(
        w_down, down_moment, down_square, grad_out
    )
    return (
        fine_precip,
        up_next,
        down_next,
        up_moment_next,
        up_square_next,
        down_moment_next,
        down_square_next,
    )


def solution(mesh):
    placed = (
        P(("dp", "expert"), None),
        P(("dp", "expert"), None),
        P(("dp", "expert"), None),
        P(),
        P(("dp", "expert")),
        P(),
        P("expert", None, "dp"),
        P("expert", "dp", None),
        P("expert", None, "dp"),
        P("expert", None, "dp"),
        P("expert", "dp", None),
        P("expert", "dp", None),
    )
    return jax.shard_map(
        local,
        mesh=mesh,
        in_specs=placed,
        out_specs=(
            P(("dp", "expert"), None),
            P("expert", None, "dp"),
            P("expert", "dp", None),
            P("expert", None, "dp"),
            P("expert", None, "dp"),
            P("expert", "dp", None),
            P("expert", "dp", None),
        ),
        check_vma=False,
    )
```

profile of v0, /device:TPU:1, one launch (start us, length us, event | category | flops | bytes accessed | tf_op | source)
XLA Modules:
  0.0 303.4 jit_solution(4484119608090613356)
XLA Ops:
  7.2 0.8 select_reduce_fusion.2
  8.0 0.8 select_reduce_fusion.1
  8.8 0.1 fusion.28
  8.9 0.2 reduce_window_sum.11
  9.1 0.2 select_reduce_fusion
  9.3 1.0 scatter_custom_fusion
  10.3 0.9 concatenate.7
  11.3 0.9 concatenate.6
  12.2 1.2 gather_fusion.2
  13.3 1.2 gather_fusion.1
  14.5 0.1 broadcast_select_fusion
  14.7 0.1 copy.29
  14.8 38.5 %all_to_all.15 = bf16[2,32,4,512]{3,2,0,1:T(4,128)(2,1)S(1)} all-to-all(bf16[2,32,4,512]{3,2,0,1:T(4,128)(2,1)S(1)} %copy.29), channel_id=1, replica_groups=mesh['dp'=16,'expert'=32] {'expert'}, dimensions={1} | all-to-all | bytes 524288 | tf_op jit(solution)/shard_map/all_to_all | solution.py:101
  53.3 0.1 copy.30
  53.4 0.8 reshape.142
  54.3 58.6 %all-gather.3.cloned.1.call-done = bf16[2,2048,512]{2,1,0:T(8,128)(2,1)} async-done(((bf16[2,128,512]{2,1,0:T(8,128)(2,1)}), bf16[2,2048,512]{2,1,0:T(8,128)(2,1)}) %all-gather.3.cloned.1.call-update) | async-done | bytes 4194320 | tf_op jit(solution)/shard_map/all_gather | solution.py:106
  112.9 3.4 %fusion.46 = f32[2,2048,128]{2,1,0:T(8,128)S(1)} fusion(bf16[2,2048,512]{2,1,0:T(8,128)(2,1)} %all-gather.3.cloned.1.call-done, bf16[2,512,128]{2,1,0:T(8,128)(2,1)S(1)} %copy-done.2), kind=kOutput, calls=%fused_computation.89 | convolution fusion | flops 536870912 | bytes 6553600 | tf_op jit(solution)/shard_map/krd,kdf->krf/dot_general | solution.py:58
  116.4 3.2 %convert_bitcast_fusion = bf16[2048,2,512]{2,0,1:T(8,128)(2,1)} fusion(bf16[2,128,512]{2,1,0:T(8,128)(2,1)S(1)} %copy-done.1, f32[2,2048,128]{2,1,0:T(8,128)S(1)} %fusion.46), kind=kOutput, calls=%fused_computation.4 | convolution fusion | flops 541589504 | bytes 6553600 | tf_op jit(solution)/shard_map/rkf,kfd->rkd/dot_general | solution.py:114
  119.7 0.1 copy.33
  119.8 34.9 %all_to_all.16 = bf16[2,32,4,512]{3,2,0,1:T(4,128)(2,1)S(1)} all-to-all(bf16[2,32,4,512]{3,2,0,1:T(4,128)(2,1)S(1)} %copy.33), channel_id=1, replica_groups=mesh['dp'=16,'expert'=32] {'expert'}, dimensions={1} | all-to-all | bytes 524288 | tf_op jit(solution)/shard_map/all_to_all | solution.py:102
  154.9 0.8 reshape.146
  155.7 55.1 %reduce-scatter.2.cloned.1.call-done = bf16[128,2,512]{2,0,1:T(8,128)(2,1)} async-done(((bf16[2048,2,512]{2,0,1:T(8,128)(2,1)}), bf16[128,2,512]{2,0,1:T(8,128)(2,1)}) %reduce-scatter.2.cloned.1.call-update) | async-done | bytes 262160 | tf_op jit(solution)/shard_map/reduce_scatter | solution.py:113
  210.8 1.0 reshape.143
  211.8 0.8 copy.31
  212.6 14.6 %all-to-all-start.1 = ((bf16[2,32,4,512]{3,2,0,1:T(4,128)(2,1)}), bf16[2,32,4,512]{3,2,0,1:T(4,128)(2,1)S(1)}, u32[]{:S(2)}, u32[]{:S(2)}) async-start(bf16[2,32,4,512]{3,2,0,1:T(4,128)(2,1)} %copy.31), calls=%async_computation.2 | async-start | bytes 524288 | tf_op jit(solution)/shard_map/all_to_all | solution.py:122
  227.3 55.6 %all-gather.5.cloned.1.call-done = bf16[2,2048,512]{2,1,0:T(8,128)(2,1)} async-done(((bf16[2,128,512]{2,1,0:T(8,128)(2,1)}), bf16[2,2048,512]{2,1,0:T(8,128)(2,1)}) %all-gather.5.cloned.1.call-update) | async-done | bytes 4194320 | tf_op jit(solution)/shard_map/all_gather | solution.py:107
  282.9 4.4 %fusion.19 = (bf16[2,128,512]{2,1,0:T(8,128)(2,1)}, bf16[2,128,512]{2,1,0:T(8,128)(2,1)}, bf16[2,128,512]{2,1,0:T(8,128)(2,1)}) fusion(bf16[2,128,512]{2,1,0:T(8,128)(2,1)S(1)} %copy-done.5, bf16[2,128,512]{2,1,0:T(8,128)(2,1)S(1)} %copy-done.6, bf16[2,128,512]{2,1,0:T(8,128)(2,1)S(1)} %copy-done.1, bf16[2,2048,512]{2,1,0:T(8,128)(2,1)} %all-gather.5.cloned.1.call-done, ...), kind=kOutput, calls=%fused_computation.35 | convolution fusion | flops 541982720 | bytes 7864320 | tf_op jit(solution)/shard_map/krf,krd->kfd/dot_general | solution.py:71
  287.3 7.5 %fusion.20 = (bf16[2,512,128]{2,1,0:T(8,128)(2,1)}, bf16[2,512,128]{2,1,0:T(8,128)(2,1)}, bf16[2,512,128]{2,1,0:T(8,128)(2,1)}) fusion(bf16[2,512,128]{2,1,0:T(8,128)(2,1)} %param.23, bf16[2,512,128]{2,1,0:T(8,128)(2,1)} %param.22, bf16[2,512,128]{2,1,0:T(8,128)(2,1)S(1)} %copy-done.2, bf16[2,2048,512]{2,1,0:T(8,128)(2,1)} %all-gather.3.cloned.1.call-done, ...), kind=kOutput, calls=%fused_computation.36 | convolution fusion | flops 1081475072 | bytes 12320768 | tf_op jit(solution)/shard_map/krd,krf->kdf/dot_general | solution.py:67
  294.7 0.1 copy.32
  294.9 0.8 gather_fusion
  295.8 0.5 fusion.45
  296.2 0.6 multiply_divide_fusion
  (32 shorter events, 0.6 us)
Async XLA Ops:
  7.2 288.6 %copy-start = (f32[512,16]{0,1:T(8,128)S(1)}, f32[512,16]{0,1:T(8,128)}, u32[]{:S(2)}) copy-start(f32[512,16]{0,1:T(8,128)} %param.19) | copy-start | bytes 98308
  7.2 105.7 %all-gather.3.cloned.1.call-start = ((), (), s32[]{:S(2)}) async-start(), calls=%async_computation.4 | async-start | bytes 4456448 | tf_op jit(solution)/shard_map/all_gather | solution.py:106
  14.5 98.4 %copy-start.2 = (bf16[2,512,128]{2,1,0:T(8,128)(2,1)S(1)}, bf16[2,512,128]{2,1,0:T(8,128)(2,1)}, u32[]{:S(2)}) copy-start(bf16[2,512,128]{2,1,0:T(8,128)(2,1)} %param.20) | copy-start | bytes 786436
  54.2 62.1 %copy-start.1 = (bf16[2,128,512]{2,1,0:T(8,128)(2,1)S(1)}, bf16[2,128,512]{2,1,0:T(8,128)(2,1)}, u32[]{:S(2)}) copy-start(bf16[2,128,512]{2,1,0:T(8,128)(2,1)} %param.21) | copy-start | bytes 786436
  54.2 156.5 %reduce-scatter.2.cloned.1.call-start = ((), (), s32[]{:S(2)}) async-start(), calls=%async_computation.5 | async-start | bytes 4456448 | tf_op jit(solution)/shard_map/reduce_scatter | solution.py:113
  119.6 163.3 %all-gather.5.cloned.1.call-start = ((), (), s32[]{:S(2)}) async-start(), calls=%async_computation.6 | async-start | bytes 4456448 | tf_op jit(solution)/shard_map/all_gather | solution.py:107
  119.7 163.2 %copy-start.5 = (bf16[2,128,512]{2,1,0:T(8,128)(2,1)S(1)}, bf16[2,128,512]{2,1,0:T(8,128)(2,1)}, u32[]{:S(2)}) copy-start(bf16[2,128,512]{2,1,0:T(8,128)(2,1)} %param.25) | copy-start | bytes 786436
  119.7 163.2 %copy-start.6 = (bf16[2,128,512]{2,1,0:T(8,128)(2,1)S(1)}, bf16[2,128,512]{2,1,0:T(8,128)(2,1)}, u32[]{:S(2)}) copy-start(bf16[2,128,512]{2,1,0:T(8,128)(2,1)} %param.24) | copy-start | bytes 786436
  212.6 82.1 %all-to-all-start.1 = ((bf16[2,32,4,512]{3,2,0,1:T(4,128)(2,1)}), bf16[2,32,4,512]{3,2,0,1:T(4,128)(2,1)S(1)}, u32[]{:S(2)}, u32[]{:S(2)}) async-start(bf16[2,32,4,512]{3,2,0,1:T(4,128)(2,1)} %copy.31), calls=%async_computation.2 | async-start | bytes 524288 | tf_op jit(solution)/shard_map/all_to_all | solution.py:122
  294.7 1.0 copy-start.3
  294.7 1.5 copy-start.4
Sparse Core Ops, SparseCore 0:
  54.4 58.5 all-gather.2
  119.7 91.0 reduce-scatter.1
  214.8 68.0 all-gather.4
where the time goes:
time: 304 us; the launch traced here: 303 us
  waiting for transfers between devices  169 us (56%)
  blocking collectives  73.5 us (24%)
  matrix products  18.9 us (6%)
  starting transfers between devices  14.8 us (5%)
  between operations  14 us (5%)
  local copies, waits for them, and re-layouts  10 us (3%)
    all_gather x1, waiting for transfers between devices, local(): piece_x = lax.all_gather(recv_x, 'dp', axis=1, tiled=True)  58.6 us
    all_gather x1, waiting for transfers between devices, local(): piece_grad = lax.all_gather(recv_grad, 'dp', axis=1, tiled=True)  55.6 us
    reduce_scatter x1, waiting for transfers between devices, local(): lax.psum_scatter(jnp.einsum('rkf,kfd->rkd', hidden_all, w_down, preferred...  55.1 us
    all_to_all x1, blocking collectives, local(): lax.all_to_all(send_x, 'expert', split_axis=1, concat_axis=1, tiled=True)  38.5 us
    all_to_all x1, blocking collectives, local(): lax.all_to_all(send_grad, 'expert', split_axis=1, concat_axis=1, tiled=True)  34.9 us
    all_to_all x1, starting transfers between devices, local(): lax.all_to_all(outgoing, 'expert', split_axis=1, concat_axis=1, tiled=True)  14.6 us
    dot_general x1, matrix products, outer_in(): jnp.einsum('krd,krf->kdf', rows_x, hidden_grad, preferred_element_type=jn...  7.45 us
  transfers between devices with their start and end apart: 4, of which 3 were waited for; matrix products, arithmetic and copies ran while one was open for 5% of the time, Pallas kernels for 0%

commit v1 on v0

--- a/solution.py
+++ b/solution.py
@@ -103,7 +103,10 @@
     )
     recv_x = recv_x.reshape(local_count, recv_rows, width)
     recv_grad = recv_grad.reshape(local_count, recv_rows, width)
-    piece_x = lax.all_gather(recv_x, "dp", axis=1, tiled=True)
+    size = lax.axis_size("dp")
+    shards = jnp.stack([recv_x for _ in range(size)])
+    shards = lax.all_to_all(shards, "dp", split_axis=0, concat_axis=0)
+    piece_x = jnp.concatenate(shards, axis=1)
     piece_grad = lax.all_gather(recv_grad, "dp", axis=1, tiled=True)
     hidden, hidden_grad = expert_rows(piece_x, piece_grad, w_up, w_down)
     grad_in = outer_in(piece_x, hidden_grad)

time: 304 us -> 292 us (0.961)
  waiting for transfers between devices: 169 us -> 110 us
  blocking collectives: 73.5 us -> 123 us
    all_gather x1 -> x0, waiting for transfers between devices: 58.6 us -> none  [local(): piece_x = lax.all_gather(recv_x, 'dp', axis=1, tiled=True)]
    all_to_all x0 -> x1, blocking collectives: none -> 56.2 us  [local(): shards = lax.all_to_all(shards, 'dp', split_axis=0, concat_axis=0)]
    all_to_all x1, blocking collectives: 34.9 us -> 27.8 us  [local(): lax.all_to_all(send_grad, 'expert', split_axis=1, concat_axis=1, tiled=True)]
  transfers between devices with their start and end apart: 4 -> 3, of which waited for: 3 -> 2; matrix products, arithmetic and copies ran while one was open for 5% -> 5% of each run, Pallas kernels for 0% -> 0%
where the time goes in v1:
time: 292 us
  blocking collectives  123 us (42%)
  waiting for transfers between devices  110 us (38%)
  matrix products  16.8 us (6%)
  starting transfers between devices  14.8 us (5%)
  between operations  14.3 us (5%)
  local copies, waits for them, and re-layouts  11 us (4%)
    all_to_all x1, blocking collectives, local(): shards = lax.all_to_all(shards, 'dp', split_axis=0, concat_axis=0)  56.2 us
    all_gather x1, waiting for transfers between devices, local(): piece_grad = lax.all_gather(recv_grad, 'dp', axis=1, tiled=True)  55.6 us
    reduce_scatter x1, waiting for transfers between devices, local(): lax.psum_scatter(jnp.einsum('rkf,kfd->rkd', hidden_all, w_down, preferred...  54.3 us
    all_to_all x1, blocking collectives, local(): lax.all_to_all(send_x, 'expert', split_axis=1, concat_axis=1, tiled=True)  38.5 us
    all_to_all x1, blocking collectives, local(): lax.all_to_all(send_grad, 'expert', split_axis=1, concat_axis=1, tiled=True)  27.8 us
    all_to_all x1, starting transfers between devices, local(): lax.all_to_all(outgoing, 'expert', split_axis=1, concat_axis=1, tiled=True)  14.7 us
    dot_general x1, matrix products, outer_in(): jnp.einsum('krd,krf->kdf', rows_x, hidden_grad, preferred_element_type=jn...  7.45 us
  transfers between devices with their start and end apart: 3, of which 2 were waited for; matrix products, arithmetic and copies ran while one was open for 5% of the time, Pallas kernels for 0%

profile of v1, /device:TPU:1, one launch (start us, length us, event | category | flops | bytes accessed | tf_op | source)
XLA Modules:
  0.0 292.0 jit_solution(16573169113692655332)
XLA Ops:
  7.2 0.8 select_reduce_fusion.2
  8.0 0.8 select_reduce_fusion.1
  8.8 0.1 fusion.28
  8.9 0.2 reduce_window_sum.11
  9.1 0.2 select_reduce_fusion
  9.3 1.0 scatter_custom_fusion
  10.3 0.9 concatenate.7
  11.3 0.9 concatenate.6
  12.2 1.2 gather_fusion.2
  13.3 1.2 gather_fusion.1
  14.5 0.1 broadcast_select_fusion
  14.8 38.5 %all_to_all.20 = bf16[2,32,4,512]{3,2,0,1:T(4,128)(2,1)S(1)} all-to-all(bf16[2,32,4,512]{3,2,0,1:T(4,128)(2,1)S(1)} %copy.39), channel_id=1, replica_groups=mesh['dp'=16,'expert'=32] {'expert'}, dimensions={1} | all-to-all | bytes 524288 | tf_op jit(solution)/shard_map/all_to_all | solution.py:101
  53.3 0.2 copy.40
  53.6 0.5 stack.3
  54.0 56.2 %all_to_all.21 = bf16[16,2,128,512]{3,2,1,0:T(8,128)(2,1)S(1)} all-to-all(bf16[16,2,128,512]{3,2,1,0:T(8,128)(2,1)S(1)} %stack.3), channel_id=1, replica_groups=mesh['dp'=16,'expert'=32] {'dp'}, dimensions={0} | all-to-all | bytes 8388608 | tf_op jit(solution)/shard_map/all_to_all | solution.py:108
  110.3 0.4 copy.42
  110.7 0.5 copy-done.3
  111.2 1.3 fusion.46
  112.5 0.2 copy-done.1
  112.6 3.2 %convert_bitcast_fusion = bf16[2048,2,512]{2,0,1:T(8,128)(2,1)} fusion(bf16[2,128,512]{2,1,0:T(8,128)(2,1)S(1)} %copy-done.2, f32[2,2048,128]{2,1,0:T(8,128)S(1)} %fusion.46), kind=kOutput, calls=%fused_computation.4 | convolution fusion | flops 541589504 | bytes 6553600 | tf_op jit(solution)/shard_map/rkf,kfd->rkd/dot_general | solution.py:117
  116.1 27.8 %all_to_all.22 = bf16[2,32,4,512]{3,2,0,1:T(4,128)(2,1)S(1)} all-to-all(bf16[2,32,4,512]{3,2,0,1:T(4,128)(2,1)S(1)} %copy.45), channel_id=1, replica_groups=mesh['dp'=16,'expert'=32] {'expert'}, dimensions={1} | all-to-all | bytes 524288 | tf_op jit(solution)/shard_map/all_to_all | solution.py:102
  144.0 0.8 reshape.152
  144.8 54.3 %reduce-scatter.2.cloned.1.call-done = bf16[128,2,512]{2,0,1:T(8,128)(2,1)} async-done(((bf16[2048,2,512]{2,0,1:T(8,128)(2,1)}), bf16[128,2,512]{2,0,1:T(8,128)(2,1)}) %reduce-scatter.2.cloned.1.call-update) | async-done | bytes 262160 | tf_op jit(solution)/shard_map/reduce_scatter | solution.py:116
  199.1 1.0 reshape.149
  200.1 0.8 copy.43
  200.9 14.7 %all-to-all-start.2 = ((bf16[2,32,4,512]{3,2,0,1:T(4,128)(2,1)}), bf16[2,32,4,512]{3,2,0,1:T(4,128)(2,1)S(1)}, u32[]{:S(2)}, u32[]{:S(2)}) async-start(bf16[2,32,4,512]{3,2,0,1:T(4,128)(2,1)} %copy.43), calls=%async_computation.3 | async-start | bytes 524288 | tf_op jit(solution)/shard_map/all_to_all | solution.py:125
  215.6 55.6 %all-gather.2.cloned.1.call-done = bf16[2,2048,512]{2,1,0:T(8,128)(2,1)} async-done(((bf16[2,128,512]{2,1,0:T(8,128)(2,1)}), bf16[2,2048,512]{2,1,0:T(8,128)(2,1)}) %all-gather.2.cloned.1.call-update) | async-done | bytes 4194320 | tf_op jit(solution)/shard_map/all_gather | solution.py:110
  271.2 4.4 %fusion.19 = (bf16[2,128,512]{2,1,0:T(8,128)(2,1)}, bf16[2,128,512]{2,1,0:T(8,128)(2,1)}, bf16[2,128,512]{2,1,0:T(8,128)(2,1)}) fusion(bf16[2,128,512]{2,1,0:T(8,128)(2,1)S(1)} %copy-done.6, bf16[2,128,512]{2,1,0:T(8,128)(2,1)S(1)} %copy-done.7, bf16[2,128,512]{2,1,0:T(8,128)(2,1)S(1)} %copy-done.2, bf16[2,2048,512]{2,1,0:T(8,128)(2,1)} %all-gather.2.cloned.1.call-done, ...), kind=kOutput, calls=%fused_computation.35 | convolution fusion | flops 541982720 | bytes 7864320 | tf_op jit(solution)/shard_map/krf,krd->kfd/dot_general | solution.py:71
  275.6 7.5 %fusion.20 = (bf16[2,512,128]{2,1,0:T(8,128)(2,1)}, bf16[2,512,128]{2,1,0:T(8,128)(2,1)}, bf16[2,512,128]{2,1,0:T(8,128)(2,1)}) fusion(bf16[2,512,128]{2,1,0:T(8,128)(2,1)} %param.23, bf16[2,512,128]{2,1,0:T(8,128)(2,1)} %param.22, bf16[2,512,128]{2,1,0:T(8,128)(2,1)S(1)} %copy-done.3, bf16[2,2048,512]{2,1,0:T(8,128)(2,1)} %bitcast.51, ...), kind=kOutput, calls=%fused_computation.36 | convolution fusion | flops 1081475072 | bytes 12320768 | tf_op jit(solution)/shard_map/krd,krf->kdf/dot_general | solution.py:67
  283.2 0.8 gather_fusion
  284.1 0.5 fusion.45
  284.5 0.6 multiply_divide_fusion
  (34 shorter events, 0.8 us)
Async XLA Ops:
  7.2 276.9 %copy-start = (f32[512,16]{0,1:T(8,128)S(1)}, f32[512,16]{0,1:T(8,128)}, u32[]{:S(2)}) copy-start(f32[512,16]{0,1:T(8,128)} %param.19) | copy-start | bytes 98308
  7.2 191.9 %reduce-scatter.2.cloned.1.call-start = ((), (), s32[]{:S(2)}) async-start(), calls=%async_computation.5 | async-start | bytes 4456448 | tf_op jit(solution)/shard_map/reduce_scatter | solution.py:116
  110.3 1.0 copy-start.3
  110.7 1.9 copy-start.1
  111.2 1.4 copy-start.2
  115.9 155.3 %all-gather.2.cloned.1.call-start = ((), (), s32[]{:S(2)}) async-start(), calls=%async_computation.6 | async-start | bytes 4456448 | tf_op jit(solution)/shard_map/all_gather | solution.py:110
  116.0 155.2 %copy-start.6 = (bf16[2,128,512]{2,1,0:T(8,128)(2,1)S(1)}, bf16[2,128,512]{2,1,0:T(8,128)(2,1)}, u32[]{:S(2)}) copy-start(bf16[2,128,512]{2,1,0:T(8,128)(2,1)} %param.25) | copy-start | bytes 786436
  116.0 155.2 %copy-start.7 = (bf16[2,128,512]{2,1,0:T(8,128)(2,1)S(1)}, bf16[2,128,512]{2,1,0:T(8,128)(2,1)}, u32[]{:S(2)}) copy-start(bf16[2,128,512]{2,1,0:T(8,128)(2,1)} %param.24) | copy-start | bytes 786436
  200.9 82.1 %all-to-all-start.2 = ((bf16[2,32,4,512]{3,2,0,1:T(4,128)(2,1)}), bf16[2,32,4,512]{3,2,0,1:T(4,128)(2,1)S(1)}, u32[]{:S(2)}, u32[]{:S(2)}) async-start(bf16[2,32,4,512]{3,2,0,1:T(4,128)(2,1)} %copy.43), calls=%async_computation.3 | async-start | bytes 524288 | tf_op jit(solution)/shard_map/all_to_all | solution.py:125
  283.0 1.0 copy-start.4
  283.0 1.5 copy-start.5
Sparse Core Ops, SparseCore 0:
  116.0 83.0 reduce-scatter.1
  203.1 68.0 all-gather.1
